TPU v7x, 512 devices: a whole 4x4x16 slice. The times are simulated.
512 devices in a mesh: grp: 16 (over y, x), tile: 32 (over z, core).
Axes of the slice: x: 4, y: 4, z: 16, core: 2. Of those that a mesh axis runs over, the one named last changes fastest.
Arguments:
- latent: bfloat16 [8, 64, 64, 512], P(None, 'grp', 'tile'), may hold values from -36 to 36
- coarse_filters: bfloat16 [3, 3, 3, 512, 512], P(None, None, None, None, 'grp'), may hold values from -0.0546875 to 0.0546875
- mid_filters: bfloat16 [3, 3, 3, 256, 256], P(None, None, None, None, 'tile'), may hold values from -0.078125 to 0.078125
- fine_filters: bfloat16 [3, 3, 3, 128, 128], replicated, may hold values from -0.109375 to 0.109375
- coarse_proj: bfloat16 [512, 256], replicated, may hold values from -0.25 to 0.25
- mid_proj: bfloat16 [256, 128], replicated, may hold values from -0.375 to 0.375
Outputs:
- frames_out: bfloat16 [8, 256, 256, 128], P(None, 'grp', 'tile')
All inputs are finite; a program needn't handle non-finite values.
Results may differ from a plain program's by a relative error of at most 0.018.
Values may be sent and summed in bfloat16 or wider, within the bound.
A program may use at most 128 MiB of HBM per device.

v0:
```python
import jax
import jax.numpy as jnp
from jax import lax
from jax.sharding import PartitionSpec as P


def with_halo(shard, sides, width):
    for axis, dim in sides:
        size, length = (lax.axis_size(axis), shard.shape[dim])
        up = [(i, (i + 1) % size) for i in range(size - 1)]
        down = [(j, i) for i, j in up]
        last = lax.slice_in_dim(shard, length - width, length, axis=dim)
        initial = lax.slice_in_dim(shard, 0, width, axis=dim)
        before = lax.ppermute(last, axis, up)
        after = lax.ppermute(initial, axis, down)
        shard = jnp.concatenate([before, shard, after], axis=dim)
    return shard


def activate(values):
    widened = values.astype(jnp.float32)
    scaled = widened * lax.rsqrt(jnp.mean(widened * widened, axis=-1, keepdims=True) + 1e-06)
    return jax.nn.silu(scaled).astype(jnp.bfloat16)


def double_size(values):
    return jnp.repeat(jnp.repeat(values, 2, axis=1), 2, axis=2)


def time_padded(values):
    return jnp.pad(values, ((2, 0), (0, 0), (0, 0), (0, 0)))


def stencil_columns(extended):
    padded = time_padded(extended)
    height = extended.shape[1] - 2
    breadth = extended.shape[2] - 2
    return jnp.concatenate(
        [
            padded[:, row_step : row_step + height, col_step : col_step + breadth, :]
            for row_step in range(3)
            for col_step in range(3)
        ],
        axis=-1,
    )


def apply_columns(columns, filters):
    frames = columns.shape[0] - 2
    folded = filters.reshape(3, 9 * filters.shape[3], filters.shape[4])
    total = jnp.dot(columns[0:frames], folded[0], preferred_element_type=jnp.float32)
    for frame_step in (1, 2):
        total = total + jnp.dot(
            columns[frame_step : frame_step + frames],
            folded[frame_step],
            preferred_element_type=jnp.float32,
        )
    return total


def coarse_conv(extended, filters):
    padded = time_padded(extended)
    frames = extended.shape[0]
    height = extended.shape[1] - 2
    breadth = extended.shape[2] - 2
    inputs = filters.shape[3]
    outputs = filters.shape[4]
    total = jnp.zeros((frames, height, breadth, outputs), jnp.float32)
    for frame_step in range(3):
        spread = jnp.transpose(filters[frame_step], (2, 0, 1, 3)).reshape(inputs, 9 * outputs)
        products = jnp.dot(
            padded[frame_step : frame_step + frames], spread, preferred_element_type=jnp.float32
        )
        for row_step in range(3):
            for col_step in range(3):
                lane = 3 * row_step + col_step
                total = (
                    total
                    + products[
                        :,
                        row_step : row_step + height,
                        col_step : col_step + breadth,
                        lane * outputs : (lane + 1) * outputs,
                    ]
                )
    return total


def middle_conv(extended, mid_filters):
    columns = stencil_columns(extended)
    return apply_columns(columns, lax.all_gather(mid_filters, "tile", axis=4, tiled=True))


def body(latent, coarse_filters, mid_filters, fine_filters, coarse_proj, mid_proj):
    first_act = activate(latent)
    whole = lax.all_gather(first_act, "grp", axis=1, tiled=True)
    widened = with_halo(whole, (("tile", 2),), 1)
    padded = jnp.pad(widened, ((0, 0), (1, 1), (0, 0), (0, 0)))
    filtered = coarse_conv(padded, coarse_filters).astype(jnp.bfloat16)
    returned = lax.all_to_all(filtered, "grp", split_axis=1, concat_axis=3, tiled=True)
    level_zero = (latent.astype(jnp.float32) + returned.astype(jnp.float32)).astype(jnp.bfloat16)
    reduced = jnp.dot(level_zero, coarse_proj, preferred_element_type=jnp.float32).astype(
        jnp.bfloat16
    )
    mid_act = double_size(activate(reduced))
    mid_ext = with_halo(mid_act, (("grp", 1), ("tile", 2)), 1)
    mid_terms = middle_conv(mid_ext, mid_filters)
    mid_out = (double_size(reduced).astype(jnp.float32) + mid_terms).astype(jnp.bfloat16)
    fine_low = jnp.dot(mid_out, mid_proj, preferred_element_type=jnp.float32).astype(jnp.bfloat16)
    fine_in = double_size(fine_low)
    fine_act = double_size(activate(fine_low))
    fine_ext = with_halo(fine_act, (("grp", 1), ("tile", 2)), 1)
    fine_terms = apply_columns(stencil_columns(fine_ext), fine_filters)
    return (fine_in.astype(jnp.float32) + fine_terms).astype(jnp.bfloat16)


def solution(mesh):
    in_specs = (
        P(None, "grp", "tile", None),
        P(None, None, None, None, "grp"),
        P(None, None, None, None, "tile"),
        P(),
        P(),
        P(),
    )
    out_specs = P(None, "grp", "tile", None)
    return jax.shard_map(body, mesh=mesh, in_specs=in_specs, out_specs=out_specs, check_vma=False)
```

profile of v0, /device:TPU:7, one launch (start us, length us, event | category | flops | bytes accessed | tf_op | source)
XLA Modules:
  0.0 200.4 jit_solution(11646952750403236550)
XLA Ops:
  6.5 1.0 fusion.34
  7.6 1.6 fusion.33
  9.3 0.7 all-gather.5.cloned.1.call-update
  10.0 61.1 %all-gather.3.cloned.1.call-done = bf16[8,64,2,512]{3,0,2,1:T(8,128)(2,1)} async-done(((bf16[8,4,2,512]{3,0,2,1:T(8,128)(2,1)}), bf16[8,64,2,512]{3,0,2,1:T(8,128)(2,1)}) %all-gather.3.cloned.1.call-update) | async-done | bytes 1048592 | tf_op jit(solution)/shard_map/all_gather | solution.py:96
  71.1 1.8 copy.25
  73.0 5.1 %collective-permute-start = (bf16[8,64,1,512]{3,1,2,0:T(8,128)(2,1)S(1)}, bf16[8,64,1,512]{3,1,2,0:T(8,128)(2,1)S(1)}, u32[]{:S(2)}, u32[]{:S(2)}) collective-permute-start(bf16[8,64,1,512]{3,1,2,0:T(8,128)(2,1)S(1)} %get-tuple-element.8), channel_id=1, source_target_pairs={{0,1},{1,2},{2,3},{3,4},{4,5},{5,6},{6,7},{7,8},{8,9},{9,10},{10,1... | collective-permute-start | bytes 1572872 | tf_op jit(solution)/shard_map/ppermute | solution.py:14
  78.0 1.9 collective-permute-start.1
  80.0 4.1 %collective-permute-done = bf16[8,64,1,512]{3,1,2,0:T(8,128)(2,1)S(1)} collective-permute-done((bf16[8,64,1,512]{3,1,2,0:T(8,128)(2,1)S(1)}, bf16[8,64,1,512]{3,1,2,0:T(8,128)(2,1)S(1)}, u32[]{:S(2)}, u32[]{:S(2)}) %collective-permute-start) | collective-permute-done | bytes 524320 | tf_op jit(solution)/shard_map/ppermute | solution.py:14
  84.1 4.4 %collective-permute-done.1 = bf16[8,64,1,512]{3,1,2,0:T(8,128)(2,1)S(1)} collective-permute-done((bf16[8,64,1,512]{3,1,2,0:T(8,128)(2,1)S(1)}, bf16[8,64,1,512]{3,1,2,0:T(8,128)(2,1)S(1)}, u32[]{:S(2)}, u32[]{:S(2)}) %collective-permute-start.1) | collective-permute-done | bytes 524320 | tf_op jit(solution)/shard_map/ppermute | solution.py:15
  88.5 1.0 fusion.5
  89.6 1.4 fusion.47
  91.0 1.4 fusion.50
  92.5 1.4 fusion.51
  93.9 2.5 %fusion.24 = bf16[8,64,2,32]{3,1,2,0:T(8,128)(2,1)S(1)} fusion(f32[8,66,4,288]{3,1,2,0:T(8,128)S(1)} %fusion.47, f32[8,66,4,288]{3,1,2,0:T(8,128)S(1)} %fusion.51, f32[8,66,4,288]{3,1,2,0:T(8,128)S(1)} %fusion.50), kind=kLoop, calls=%fused_computation.35 | loop fusion | flops 884736 | bytes 3604480 | tf_op jit(solution)/shard_map/convert_element_type | solution.py:99
  96.4 0.3 copy.67
  96.7 0.3 reshape.91
  97.0 9.8 %all_to_all.4 = bf16[16,2,1024]{2,1,0:T(2,128)(2,1)S(1)} all-to-all(bf16[16,2,1024]{2,1,0:T(2,128)(2,1)S(1)} %reshape.91), channel_id=1, replica_groups=mesh['grp'=16,'tile'=32] {'grp'}, dimensions={0} | all-to-all | bytes 131072 | tf_op jit(solution)/shard_map/all_to_all | solution.py:100
  106.7 0.2 reshape.92
  106.9 0.2 copy.66
  107.1 0.2 reshape.78
  107.3 0.3 multiply_reduce_fusion.1
  108.0 3.7 %collective-permute-start.2 = (bf16[8,1,4,256]{3,2,1,0:T(4,128)(2,1)S(1)}, bf16[8,1,4,256]{3,2,1,0:T(4,128)(2,1)S(1)}, u32[]{:S(2)}, u32[]{:S(2)}) collective-permute-start(bf16[8,1,4,256]{3,2,1,0:T(4,128)(2,1)S(1)} %get-tuple-element.23), channel_id=1, source_target_pairs={{0,32},{32,64},{64,96},{96,128},{128,160},{160,192},{192,224},{224... | collective-permute-start | bytes 49160 | tf_op jit(solution)/shard_map/ppermute | solution.py:14
  111.7 1.9 collective-permute-start.3
  113.7 4.6 %collective-permute-done.3 = bf16[8,1,4,256]{3,2,1,0:T(4,128)(2,1)S(1)} collective-permute-done((bf16[8,1,4,256]{3,2,1,0:T(4,128)(2,1)S(1)}, bf16[8,1,4,256]{3,2,1,0:T(4,128)(2,1)S(1)}, u32[]{:S(2)}, u32[]{:S(2)}) %collective-permute-start.3) | collective-permute-done | bytes 16416 | tf_op jit(solution)/shard_map/ppermute | solution.py:15
  118.4 4.6 %collective-permute-start.4 = (bf16[8,10,1,256]{3,2,1,0:T(2,128)(2,1)S(1)}, bf16[8,10,1,256]{3,2,1,0:T(2,128)(2,1)S(1)}, u32[]{:S(2)}, u32[]{:S(2)}) collective-permute-start(bf16[8,10,1,256]{3,2,1,0:T(2,128)(2,1)S(1)} %get-tuple-element.20), channel_id=1, source_target_pairs={{0,1},{1,2},{2,3},{3,4},{4,5},{5,6},{6,7},{7,8},{8,9},{9,10},{10,1... | collective-permute-start | bytes 122888 | tf_op jit(solution)/shard_map/ppermute | solution.py:14
  123.1 2.1 %collective-permute-start.5 = (bf16[8,10,1,256]{3,2,1,0:T(2,128)(2,1)S(1)}, bf16[8,10,1,256]{3,2,1,0:T(2,128)(2,1)S(1)}, u32[]{:S(2)}, u32[]{:S(2)}) collective-permute-start(bf16[8,10,1,256]{3,2,1,0:T(2,128)(2,1)S(1)} %get-tuple-element.21), channel_id=1, source_target_pairs={{1,0},{2,1},{3,2},{4,3},{5,4},{6,5},{7,6},{8,7},{9,8},{10,9},{11,1... | collective-permute-start | bytes 122888 | tf_op jit(solution)/shard_map/ppermute | solution.py:15
  125.4 0.2 convert_element_type.86
  125.6 3.7 %collective-permute-done.5 = bf16[8,10,1,256]{3,2,1,0:T(2,128)(2,1)S(1)} collective-permute-done((bf16[8,10,1,256]{3,2,1,0:T(2,128)(2,1)S(1)}, bf16[8,10,1,256]{3,2,1,0:T(2,128)(2,1)S(1)}, u32[]{:S(2)}, u32[]{:S(2)}) %collective-permute-start.5) | collective-permute-done | bytes 40992 | tf_op jit(solution)/shard_map/ppermute | solution.py:15
  129.3 0.3 fusion.26
  129.6 0.7 slice_dynamic-update-slice_fusion.17
  130.4 0.8 slice_dynamic-update-slice_fusion.16
  131.2 0.8 slice_dynamic-update-slice_fusion.15
  132.0 0.8 slice_dynamic-update-slice_fusion.14
  132.8 0.8 slice_dynamic-update-slice_fusion.13
  133.6 0.8 slice_dynamic-update-slice_fusion.12
  134.4 0.8 slice_dynamic-update-slice_fusion.11
  135.2 0.8 slice_dynamic-update-slice_fusion.10
  136.0 0.8 slice_dynamic-update-slice_fusion.9
  136.8 16.2 %all-gather.5.cloned.1.call-done = bf16[3,3,3,256,256]{3,4,2,1,0:T(8,128)(2,1)} async-done(((bf16[3,3,3,256,8]{3,4,2,1,0:T(8,128)(2,1)}), bf16[3,3,3,256,256]{3,4,2,1,0:T(8,128)(2,1)}) %all-gather.5.cloned.1.call-update) | async-done | bytes 3538960 | tf_op jit(solution)/shard_map/all_gather | solution.py:91
  153.0 3.3 %fusion.40 = (bf16[1,3,3,256,256]{3,4,2,1,0:T(8,128)(2,1)S(1)}, bf16[1,3,3,256,256]{3,4,2,1,0:T(8,128)(2,1)S(1)}, bf16[1,3,3,256,256]{3,4,2,1,0:T(8,128)(2,1)}) fusion(bf16[3,3,3,256,256]{3,4,2,1,0:T(8,128)(2,1)} %all-gather.5.cloned.1.call-done), kind=kLoop, calls=%fused_computation.110 | loop fusion | bytes 7077888 | tf_op jit(solution)/shard_map/slice | solution.py:55
  156.3 2.4 %copy.49 = bf16[1,3,3,256,256]{4,3,2,1,0:T(8,128)(2,1)} copy(bf16[1,3,3,256,256]{3,4,2,1,0:T(8,128)(2,1)} %get-tuple-element.7) | data formatting | bytes 2359296
  158.7 1.6 copy.50
  160.2 0.7 copy.51
  161.0 2.4 %fusion.48 = f32[8,8,4,256]{3,2,1,0:T(4,128)S(1)} fusion(bf16[10,8,4,2304]{3,2,1,0:T(4,128)(2,1)} %slice_dynamic-update-slice_fusion.9, bf16[2304,256,1,1]{1,0,3,2:T(8,128)(2,1)} %bitcast.115), kind=kOutput, calls=%fused_computation.119 | convolution fusion | flops 301989888 | bytes 2916352 | tf_op jit(solution)/shard_map/dot_general | solution.py:51
  163.4 2.0 convolution_add_fusion.3
  165.4 2.1 %fusion.14 = bf16[8,8,4,256]{3,2,1,0:T(4,128)(2,1)S(1)} fusion(f32[8,8,4,256]{3,2,1,0:T(4,128)S(1)} %convert_element_type.86, f32[8,8,4,256]{3,2,1,0:T(4,128)S(1)} %convolution_add_fusion.3, bf16[10,8,4,2304]{3,2,1,0:T(4,128)(2,1)} %slice_dynamic-update-slice_fusion.9, bf16[2304,256,1,1]{1,0,3,2:T(8,128)(2,1)S(1)} %bitcast.114), kind=kOutput, calls=%fused_computation.21 | convolution fusion | flops 302186496 | bytes 3309568 | tf_op jit(solution)/shard_map/dot_general | solution.py:53
  167.5 0.3 multiply_reduce_fusion
  168.0 0.2 broadcast_in_dim.34
  168.2 2.7 %collective-permute-start.6 = (bf16[8,1,8,128]{3,2,1,0:T(8,128)(2,1)S(1)}, bf16[8,1,8,128]{3,2,1,0:T(8,128)(2,1)S(1)}, u32[]{:S(2)}, u32[]{:S(2)}) collective-permute-start(bf16[8,1,8,128]{3,2,1,0:T(8,128)(2,1)S(1)} %get-tuple-element.18), channel_id=1, source_target_pairs={{0,32},{32,64},{64,96},{96,128},{128,160},{160,192},{192,224},{224... | collective-permute-start | bytes 49160 | tf_op jit(solution)/shard_map/ppermute | solution.py:14
  170.9 2.6 %collective-permute-start.7 = (bf16[8,1,8,128]{3,2,1,0:T(8,128)(2,1)S(1)}, bf16[8,1,8,128]{3,2,1,0:T(8,128)(2,1)S(1)}, u32[]{:S(2)}, u32[]{:S(2)}) collective-permute-start(bf16[8,1,8,128]{3,2,1,0:T(8,128)(2,1)S(1)} %get-tuple-element.19), channel_id=1, source_target_pairs={{32,0},{64,32},{96,64},{128,96},{160,128},{192,160},{224,192},{256... | collective-permute-start | bytes 49160 | tf_op jit(solution)/shard_map/ppermute | solution.py:15
  173.5 4.0 %collective-permute-done.7 = bf16[8,1,8,128]{3,2,1,0:T(8,128)(2,1)S(1)} collective-permute-done((bf16[8,1,8,128]{3,2,1,0:T(8,128)(2,1)S(1)}, bf16[8,1,8,128]{3,2,1,0:T(8,128)(2,1)S(1)}, u32[]{:S(2)}, u32[]{:S(2)}) %collective-permute-start.7) | collective-permute-done | bytes 16416 | tf_op jit(solution)/shard_map/ppermute | solution.py:15
  177.6 5.2 %collective-permute-start.8 = (bf16[8,18,1,128]{3,2,1,0:T(2,128)(2,1)S(1)}, bf16[8,18,1,128]{3,2,1,0:T(2,128)(2,1)S(1)}, u32[]{:S(2)}, u32[]{:S(2)}) collective-permute-start(bf16[8,18,1,128]{3,2,1,0:T(2,128)(2,1)S(1)} %get-tuple-element.16), channel_id=1, source_target_pairs={{0,1},{1,2},{2,3},{3,4},{4,5},{5,6},{6,7},{7,8},{8,9},{9,10},{10,1... | collective-permute-start | bytes 110600 | tf_op jit(solution)/shard_map/ppermute | solution.py:14
  182.9 1.9 collective-permute-start.9
  184.9 3.6 %collective-permute-done.9 = bf16[8,18,1,128]{3,2,1,0:T(2,128)(2,1)S(1)} collective-permute-done((bf16[8,18,1,128]{3,2,1,0:T(2,128)(2,1)S(1)}, bf16[8,18,1,128]{3,2,1,0:T(2,128)(2,1)S(1)}, u32[]{:S(2)}, u32[]{:S(2)}) %collective-permute-start.9) | collective-permute-done | bytes 36896 | tf_op jit(solution)/shard_map/ppermute | solution.py:15
  188.5 0.4 fusion.21
  189.0 0.2 slice_dynamic-update-slice_fusion.7
  189.1 0.2 slice_dynamic-update-slice_fusion.6
  189.4 0.2 slice_dynamic-update-slice_fusion.4
  189.6 0.2 slice_dynamic-update-slice_fusion.3
  189.9 0.1 slice_dynamic-update-slice_fusion.1
  190.2 0.8 fusion.49
  191.0 0.8 convolution_add_fusion.1
  191.8 0.2 broadcast_in_dim.32
  192.0 1.5 fusion.12
  (49 shorter events, 1.9 us)
Async XLA Ops:
  6.5 100.8 %copy-start = (bf16[512,256]{1,0:T(8,128)(2,1)S(1)}, bf16[512,256]{1,0:T(8,128)(2,1)}, u32[]{:S(2)}) copy-start(bf16[512,256]{1,0:T(8,128)(2,1)} %param.10) | copy-start | bytes 786436
  6.5 73.4 %copy-start.2 = (bf16[3,3,3,512,32]{3,4,2,1,0:T(8,128)(2,1)S(1)}, bf16[3,3,3,512,32]{3,4,2,1,0:T(8,128)(2,1)}, u32[]{:S(2)}) copy-start(bf16[3,3,3,512,32]{3,4,2,1,0:T(8,128)(2,1)} %param.7) | copy-start | bytes 2654212
  6.5 64.5 %all-gather.3.cloned.1.call-start = ((), (), s32[]{:S(2)}) async-start(), calls=%async_computation.1 | async-start | bytes 1114112 | tf_op jit(solution)/shard_map/all_gather | solution.py:96
  9.2 143.8 %all-gather.5.cloned.1.call-start = ((), (), s32[]{:S(2)}) async-start(), calls=%async_computation.2 | async-start | bytes 3649536 | tf_op jit(solution)/shard_map/all_gather | solution.py:91
  73.0 11.2 %collective-permute-start = (bf16[8,64,1,512]{3,1,2,0:T(8,128)(2,1)S(1)}, bf16[8,64,1,512]{3,1,2,0:T(8,128)(2,1)S(1)}, u32[]{:S(2)}, u32[]{:S(2)}) collective-permute-start(bf16[8,64,1,512]{3,1,2,0:T(8,128)(2,1)S(1)} %get-tuple-element.8), channel_id=1, source_target_pairs={{0,1},{1,2},{2,3},{3,4},{4,5},{5,6},{6,7},{7,8},{8,9},{9,10},{10,1... | collective-permute-start | bytes 1572872 | tf_op jit(solution)/shard_map/ppermute | solution.py:14
  78.0 10.5 %collective-permute-start.1 = (bf16[8,64,1,512]{3,1,2,0:T(8,128)(2,1)S(1)}, bf16[8,64,1,512]{3,1,2,0:T(8,128)(2,1)S(1)}, u32[]{:S(2)}, u32[]{:S(2)}) collective-permute-start(bf16[8,64,1,512]{3,1,2,0:T(8,128)(2,1)S(1)} %get-tuple-element.9), channel_id=1, source_target_pairs={{1,0},{2,1},{3,2},{4,3},{5,4},{6,5},{7,6},{8,7},{9,8},{10,9},{11,1... | collective-permute-start | bytes 1572872 | tf_op jit(solution)/shard_map/ppermute | solution.py:15
  96.4 10.9 %copy-start.4 = (bf16[8,4,2,512]{3,2,1,0:T(2,128)(2,1)S(1)}, bf16[8,4,2,512]{3,2,1,0:T(2,128)(2,1)}, u32[]{:S(2)}) copy-start(bf16[8,4,2,512]{3,2,1,0:T(2,128)(2,1)} %param.6) | copy-start | bytes 196612
  108.0 5.6 %collective-permute-start.2 = (bf16[8,1,4,256]{3,2,1,0:T(4,128)(2,1)S(1)}, bf16[8,1,4,256]{3,2,1,0:T(4,128)(2,1)S(1)}, u32[]{:S(2)}, u32[]{:S(2)}) collective-permute-start(bf16[8,1,4,256]{3,2,1,0:T(4,128)(2,1)S(1)} %get-tuple-element.23), channel_id=1, source_target_pairs={{0,32},{32,64},{64,96},{96,128},{128,160},{160,192},{192,224},{224... | collective-permute-start | bytes 49160 | tf_op jit(solution)/shard_map/ppermute | solution.py:14
  111.7 6.6 %collective-permute-start.3 = (bf16[8,1,4,256]{3,2,1,0:T(4,128)(2,1)S(1)}, bf16[8,1,4,256]{3,2,1,0:T(4,128)(2,1)S(1)}, u32[]{:S(2)}, u32[]{:S(2)}) collective-permute-start(bf16[8,1,4,256]{3,2,1,0:T(4,128)(2,1)S(1)} %get-tuple-element.22), channel_id=1, source_target_pairs={{32,0},{64,32},{96,64},{128,96},{160,128},{192,160},{224,192},{256... | collective-permute-start | bytes 49160 | tf_op jit(solution)/shard_map/ppermute | solution.py:15
  118.4 7.2 %collective-permute-start.4 = (bf16[8,10,1,256]{3,2,1,0:T(2,128)(2,1)S(1)}, bf16[8,10,1,256]{3,2,1,0:T(2,128)(2,1)S(1)}, u32[]{:S(2)}, u32[]{:S(2)}) collective-permute-start(bf16[8,10,1,256]{3,2,1,0:T(2,128)(2,1)S(1)} %get-tuple-element.20), channel_id=1, source_target_pairs={{0,1},{1,2},{2,3},{3,4},{4,5},{5,6},{6,7},{7,8},{8,9},{9,10},{10,1... | collective-permute-start | bytes 122888 | tf_op jit(solution)/shard_map/ppermute | solution.py:14
  123.1 6.3 %collective-permute-start.5 = (bf16[8,10,1,256]{3,2,1,0:T(2,128)(2,1)S(1)}, bf16[8,10,1,256]{3,2,1,0:T(2,128)(2,1)S(1)}, u32[]{:S(2)}, u32[]{:S(2)}) collective-permute-start(bf16[8,10,1,256]{3,2,1,0:T(2,128)(2,1)S(1)} %get-tuple-element.21), channel_id=1, source_target_pairs={{1,0},{2,1},{3,2},{4,3},{5,4},{6,5},{7,6},{8,7},{9,8},{10,9},{11,1... | collective-permute-start | bytes 122888 | tf_op jit(solution)/shard_map/ppermute | solution.py:15
  161.0 2.4 %copy-start.1 = (bf16[1,3,3,256,256]{4,3,2,1,0:T(8,128)(2,1)S(1)}, bf16[1,3,3,256,256]{4,3,2,1,0:T(8,128)(2,1)}, u32[]{:S(2)}) copy-start(bf16[1,3,3,256,256]{4,3,2,1,0:T(8,128)(2,1)} %copy.50) | copy-start | bytes 3538948
  165.4 2.1 %copy-start.5 = (bf16[256,128]{1,0:T(8,128)(2,1)S(1)}, bf16[256,128]{1,0:T(8,128)(2,1)}, u32[]{:S(2)}) copy-start(bf16[256,128]{1,0:T(8,128)(2,1)} %param.11) | copy-start | bytes 196612
  165.4 19.4 %copy-start.3 = (bf16[3,3,3,128,128]{4,3,2,1,0:T(8,128)(2,1)S(1)}, bf16[3,3,3,128,128]{4,3,2,1,0:T(8,128)(2,1)}, u32[]{:S(2)}) copy-start(bf16[3,3,3,128,128]{4,3,2,1,0:T(8,128)(2,1)} %param.9) | copy-start | bytes 2654212
  168.2 5.3 %collective-permute-start.6 = (bf16[8,1,8,128]{3,2,1,0:T(8,128)(2,1)S(1)}, bf16[8,1,8,128]{3,2,1,0:T(8,128)(2,1)S(1)}, u32[]{:S(2)}, u32[]{:S(2)}) collective-permute-start(bf16[8,1,8,128]{3,2,1,0:T(8,128)(2,1)S(1)} %get-tuple-element.18), channel_id=1, source_target_pairs={{0,32},{32,64},{64,96},{96,128},{128,160},{160,192},{192,224},{224... | collective-permute-start | bytes 49160 | tf_op jit(solution)/shard_map/ppermute | solution.py:14
  170.9 6.6 %collective-permute-start.7 = (bf16[8,1,8,128]{3,2,1,0:T(8,128)(2,1)S(1)}, bf16[8,1,8,128]{3,2,1,0:T(8,128)(2,1)S(1)}, u32[]{:S(2)}, u32[]{:S(2)}) collective-permute-start(bf16[8,1,8,128]{3,2,1,0:T(8,128)(2,1)S(1)} %get-tuple-element.19), channel_id=1, source_target_pairs={{32,0},{64,32},{96,64},{128,96},{160,128},{192,160},{224,192},{256... | collective-permute-start | bytes 49160 | tf_op jit(solution)/shard_map/ppermute | solution.py:15
  177.6 7.3 %collective-permute-start.8 = (bf16[8,18,1,128]{3,2,1,0:T(2,128)(2,1)S(1)}, bf16[8,18,1,128]{3,2,1,0:T(2,128)(2,1)S(1)}, u32[]{:S(2)}, u32[]{:S(2)}) collective-permute-start(bf16[8,18,1,128]{3,2,1,0:T(2,128)(2,1)S(1)} %get-tuple-element.16), channel_id=1, source_target_pairs={{0,1},{1,2},{2,3},{3,4},{4,5},{5,6},{6,7},{7,8},{8,9},{9,10},{10,1... | collective-permute-start | bytes 110600 | tf_op jit(solution)/shard_map/ppermute | solution.py:14
  182.9 5.7 %collective-permute-start.9 = (bf16[8,18,1,128]{3,2,1,0:T(2,128)(2,1)S(1)}, bf16[8,18,1,128]{3,2,1,0:T(2,128)(2,1)S(1)}, u32[]{:S(2)}, u32[]{:S(2)}) collective-permute-start(bf16[8,18,1,128]{3,2,1,0:T(2,128)(2,1)S(1)} %get-tuple-element.17), channel_id=1, source_target_pairs={{1,0},{2,1},{3,2},{4,3},{5,4},{6,5},{7,6},{8,7},{9,8},{10,9},{11,1... | collective-permute-start | bytes 110600 | tf_op jit(solution)/shard_map/ppermute | solution.py:15
Sparse Core Ops, SparseCore 0:
  10.4 60.6 all-gather.2
  73.1 79.7 all-gather.4
where the time goes:
time: 201 us; the launch traced here: 200 us
  waiting for transfers between devices  102 us (51%)
  starting transfers between devices  31.8 us (16%)
  local copies, waits for them, and re-layouts  20.9 us (10%)
  matrix products  14.4 us (7%)
  between operations  13.9 us (7%)
  blocking collectives  9.77 us (5%)
  other arithmetic  7.18 us (4%)
    all_gather x1, waiting for transfers between devices, body(): whole = lax.all_gather(first_act, 'grp', axis=1, tiled=True)  61.1 us
    ppermute x5, starting transfers between devices, with_halo(): before = lax.ppermute(last, axis, up)  21.3 us
    ppermute x5, waiting for transfers between devices, with_halo(): after = lax.ppermute(initial, axis, down)  20.3 us
    all_gather x1, waiting for transfers between devices, middle_conv(): lax.all_gather(mid_filters, 'tile', axis=4, tiled=True)  16.2 us
    unnamed x35, local copies, waits for them, and re-layouts  12.7 us
    ppermute x5, starting transfers between devices, with_halo(): after = lax.ppermute(initial, axis, down)  10.5 us
    all_to_all x1, blocking collectives, body(): lax.all_to_all(filtered, 'grp', split_axis=1, concat_axis=3, tiled=True)  9.77 us
    dot_general x4, matrix products, apply_columns(): jnp.dot(columns[frame_step:frame_step + frames], folded[frame_step], pref...  6.33 us
  transfers between devices with their start and end apart: 12, of which 8 were waited for; matrix products, arithmetic and copies ran while one was open for 10% of the time, Pallas kernels for 0%

commit v1 on v0

--- a/solution.py
+++ b/solution.py
@@ -2,6 +2,17 @@
 import jax.numpy as jnp
 from jax import lax
 from jax.sharding import PartitionSpec as P
+
+
+def in_blocks(x, dim, size):
+    before, after = (x.shape[:dim], x.shape[dim + 1 :])
+    return jnp.moveaxis(x.reshape(*before, size, -1, *after), dim, 0)
+
+
+def laid_out(blocks, dim):
+    blocks = jnp.moveaxis(blocks, 0, dim)
+    lengths = blocks.shape
+    return blocks.reshape(*lengths[:dim], lengths[dim] * lengths[dim + 1], *lengths[dim + 2 :])
 
 
 def with_halo(shard, sides, width):
@@ -97,7 +108,14 @@
     widened = with_halo(whole, (("tile", 2),), 1)
     padded = jnp.pad(widened, ((0, 0), (1, 1), (0, 0), (0, 0)))
     filtered = coarse_conv(padded, coarse_filters).astype(jnp.bfloat16)
-    returned = lax.all_to_all(filtered, "grp", split_axis=1, concat_axis=3, tiled=True)
+    size_2, index = (lax.axis_size("grp"), lax.axis_index("grp"))
+    blocks = in_blocks(filtered, 1, size_2)
+    finished = [blocks[index]]
+    for turn in range(1, size_2):
+        sent = blocks[index ^ turn]
+        finished.append(lax.ppermute(sent, "grp", [(i_2, i_2 ^ turn) for i_2 in range(size_2)]))
+    blocks = jnp.stack(finished)[index ^ jnp.arange(size_2)]
+    returned = laid_out(blocks, 3)
     level_zero = (latent.astype(jnp.float32) + returned.astype(jnp.float32)).astype(jnp.bfloat16)
     reduced = jnp.dot(level_zero, coarse_proj, preferred_element_type=jnp.float32).astype(
         jnp.bfloat16

time: 201 us -> 240 us (1.19)
  the two profiles are of different devices: /device:TPU:7 before, /device:TPU:152 now
where the time goes in v1:
time: 240 us; the launch traced here: 239 us
  waiting for transfers between devices  90.4 us (38%)
  starting transfers between devices  89.3 us (37%)
  local copies, waits for them, and re-layouts  22.2 us (9%)
  between operations  15.9 us (7%)
  matrix products  14.4 us (6%)
  other arithmetic  7.2 us (3%)
    all_gather x1, waiting for transfers between devices, body(): whole = lax.all_gather(first_act, 'grp', axis=1, tiled=True)  61.4 us
    ppermute x15, starting transfers between devices, body(): lax.ppermute(sent, 'grp', [(i_2, i_2 ^ turn) for i_2 in range(size_2)])  59.9 us
    ppermute x5, waiting for transfers between devices, with_halo(): before = lax.ppermute(last, axis, up)  19 us
    ppermute x5, starting transfers between devices, with_halo(): after = lax.ppermute(initial, axis, down)  18.1 us
    unnamed x48, local copies, waits for them, and re-layouts  12.2 us
    ppermute x5, starting transfers between devices, with_halo(): before = lax.ppermute(last, axis, up)  11.2 us
    dot_general x4, matrix products, apply_columns(): jnp.dot(columns[frame_step:frame_step + frames], folded[frame_step], pref...  6.32 us
    ppermute x5, waiting for transfers between devices, with_halo(): after = lax.ppermute(initial, axis, down)  5.71 us
  transfers between devices with their start and end apart: 27, of which 8 were waited for; matrix products, arithmetic and copies ran while one was open for 8% of the time, Pallas kernels for 0%

profile of v1, /device:TPU:152, one launch (start us, length us, event | category | flops | bytes accessed | tf_op | source)
XLA Modules:
  0.0 239.4 jit_solution(16670165172685220320)
XLA Ops:
  7.4 1.0 fusion.34
  8.4 1.6 fusion.33
  10.1 61.4 %all-gather.3.cloned.1.call-done = bf16[8,64,2,512]{3,0,2,1:T(8,128)(2,1)} async-done(((bf16[8,4,2,512]{3,0,2,1:T(8,128)(2,1)}), bf16[8,64,2,512]{3,0,2,1:T(8,128)(2,1)}) %all-gather.3.cloned.1.call-update) | async-done | bytes 1048592 | tf_op jit(solution)/shard_map/all_gather | solution.py:107
  71.5 1.8 copy.68
  73.3 1.1 fusion.42
  74.4 1.9 collective-permute-start.1
  76.3 2.4 %collective-permute-start = (bf16[8,64,1,512]{3,1,2,0:T(8,128)(2,1)}, bf16[8,64,1,512]{3,1,2,0:T(8,128)(2,1)S(1)}, u32[]{:S(2)}, u32[]{:S(2)}) collective-permute-start(bf16[8,64,1,512]{3,1,2,0:T(8,128)(2,1)} %get-tuple-element.8), channel_id=1, source_target_pairs={{0,1},{1,2},{2,3},{3,4},{4,5},{5,6},{6,7},{7,8},{8,9},{9,10},{10,1... | collective-permute-start | bytes 1572872 | tf_op jit(solution)/shard_map/ppermute | solution.py:25
  78.9 4.4 %collective-permute-done.1 = bf16[8,64,1,512]{3,1,2,0:T(8,128)(2,1)S(1)} collective-permute-done((bf16[8,64,1,512]{3,1,2,0:T(8,128)(2,1)}, bf16[8,64,1,512]{3,1,2,0:T(8,128)(2,1)S(1)}, u32[]{:S(2)}, u32[]{:S(2)}) %collective-permute-start.1) | collective-permute-done | bytes 524320 | tf_op jit(solution)/shard_map/ppermute | solution.py:26
  83.3 4.9 %collective-permute-done = bf16[8,64,1,512]{3,1,2,0:T(8,128)(2,1)S(1)} collective-permute-done((bf16[8,64,1,512]{3,1,2,0:T(8,128)(2,1)}, bf16[8,64,1,512]{3,1,2,0:T(8,128)(2,1)S(1)}, u32[]{:S(2)}, u32[]{:S(2)}) %collective-permute-start) | collective-permute-done | bytes 524320 | tf_op jit(solution)/shard_map/ppermute | solution.py:25
  88.2 1.0 fusion.5
  89.3 1.4 fusion.48
  90.7 1.4 fusion.52
  92.1 1.4 fusion.51
  93.6 2.5 %fusion.24 = bf16[8,64,2,32]{3,1,2,0:T(8,128)(2,1)S(1)} fusion(f32[8,66,4,288]{3,1,2,0:T(8,128)S(1)} %fusion.48, f32[8,66,4,288]{3,1,2,0:T(8,128)S(1)} %fusion.52, f32[8,66,4,288]{3,1,2,0:T(8,128)S(1)} %fusion.51), kind=kLoop, calls=%fused_computation.36 | loop fusion | flops 884736 | bytes 3604480 | tf_op jit(solution)/shard_map/convert_element_type | solution.py:110
  96.3 2.2 collective-permute-start.2
  98.5 4.1 %collective-permute-start.3 = (bf16[8,4,2,32]{3,0,2,1:T(8,128)(2,1)S(1)}, bf16[8,4,2,32]{3,0,2,1:T(8,128)(2,1)S(1)}, u32[]{:S(2)}, u32[]{:S(2)}) collective-permute-start(bf16[8,4,2,32]{3,0,2,1:T(8,128)(2,1)S(1)} %bitcast.212), channel_id=1, source_target_pairs={{0,64},{32,96},{64,0},{96,32},{128,192},{160,224},{192,128},{224,1... | collective-permute-start | bytes 12296 | tf_op jit(solution)/shard_map/ppermute | solution.py:116
  102.6 4.2 %collective-permute-start.4 = (bf16[8,4,2,32]{3,0,2,1:T(8,128)(2,1)S(1)}, bf16[8,4,2,32]{3,0,2,1:T(8,128)(2,1)S(1)}, u32[]{:S(2)}, u32[]{:S(2)}) collective-permute-start(bf16[8,4,2,32]{3,0,2,1:T(8,128)(2,1)S(1)} %bitcast.211), channel_id=1, source_target_pairs={{0,96},{32,64},{64,32},{96,0},{128,224},{160,192},{192,160},{224,1... | collective-permute-start | bytes 12296 | tf_op jit(solution)/shard_map/ppermute | solution.py:116
  106.8 2.6 %collective-permute-start.5 = (bf16[8,4,2,32]{3,0,2,1:T(8,128)(2,1)S(1)}, bf16[8,4,2,32]{3,0,2,1:T(8,128)(2,1)S(1)}, u32[]{:S(2)}, u32[]{:S(2)}) collective-permute-start(bf16[8,4,2,32]{3,0,2,1:T(8,128)(2,1)S(1)} %bitcast.210), channel_id=1, source_target_pairs={{0,128},{32,160},{64,192},{96,224},{128,0},{160,32},{192,64},{224,... | collective-permute-start | bytes 12296 | tf_op jit(solution)/shard_map/ppermute | solution.py:116
  109.4 1.9 collective-permute-start.6
  111.5 5.6 %collective-permute-start.7 = (bf16[8,4,2,32]{3,0,2,1:T(8,128)(2,1)S(1)}, bf16[8,4,2,32]{3,0,2,1:T(8,128)(2,1)S(1)}, u32[]{:S(2)}, u32[]{:S(2)}) collective-permute-start(bf16[8,4,2,32]{3,0,2,1:T(8,128)(2,1)S(1)} %bitcast.208), channel_id=1, source_target_pairs={{0,192},{32,224},{64,128},{96,160},{128,64},{160,96},{192,0},{224,... | collective-permute-start | bytes 12296 | tf_op jit(solution)/shard_map/ppermute | solution.py:116
  117.1 4.6 %collective-permute-start.8 = (bf16[8,4,2,32]{3,0,2,1:T(8,128)(2,1)S(1)}, bf16[8,4,2,32]{3,0,2,1:T(8,128)(2,1)S(1)}, u32[]{:S(2)}, u32[]{:S(2)}) collective-permute-start(bf16[8,4,2,32]{3,0,2,1:T(8,128)(2,1)S(1)} %bitcast.207), channel_id=1, source_target_pairs={{0,224},{32,192},{64,160},{96,128},{128,96},{160,64},{192,32},{224... | collective-permute-start | bytes 12296 | tf_op jit(solution)/shard_map/ppermute | solution.py:116
  121.7 3.4 %collective-permute-start.9 = (bf16[8,4,2,32]{3,0,2,1:T(8,128)(2,1)S(1)}, bf16[8,4,2,32]{3,0,2,1:T(8,128)(2,1)S(1)}, u32[]{:S(2)}, u32[]{:S(2)}) collective-permute-start(bf16[8,4,2,32]{3,0,2,1:T(8,128)(2,1)S(1)} %bitcast.206), channel_id=1, source_target_pairs={{0,256},{32,288},{64,320},{96,352},{128,384},{160,416},{192,448},{... | collective-permute-start | bytes 12296 | tf_op jit(solution)/shard_map/ppermute | solution.py:116
  125.1 1.9 collective-permute-start.10
  127.1 7.2 %collective-permute-start.11 = (bf16[8,4,2,32]{3,0,2,1:T(8,128)(2,1)S(1)}, bf16[8,4,2,32]{3,0,2,1:T(8,128)(2,1)S(1)}, u32[]{:S(2)}, u32[]{:S(2)}) collective-permute-start(bf16[8,4,2,32]{3,0,2,1:T(8,128)(2,1)S(1)} %bitcast.204), channel_id=1, source_target_pairs={{0,320},{32,352},{64,256},{96,288},{128,448},{160,480},{192,384},{... | collective-permute-start | bytes 12296 | tf_op jit(solution)/shard_map/ppermute | solution.py:116
  134.3 5.2 %collective-permute-start.12 = (bf16[8,4,2,32]{3,0,2,1:T(8,128)(2,1)S(1)}, bf16[8,4,2,32]{3,0,2,1:T(8,128)(2,1)S(1)}, u32[]{:S(2)}, u32[]{:S(2)}) collective-permute-start(bf16[8,4,2,32]{3,0,2,1:T(8,128)(2,1)S(1)} %bitcast.203), channel_id=1, source_target_pairs={{0,352},{32,320},{64,288},{96,256},{128,480},{160,448},{192,416},{... | collective-permute-start | bytes 12296 | tf_op jit(solution)/shard_map/ppermute | solution.py:116
  139.6 2.9 %collective-permute-start.13 = (bf16[8,4,2,32]{3,0,2,1:T(8,128)(2,1)S(1)}, bf16[8,4,2,32]{3,0,2,1:T(8,128)(2,1)S(1)}, u32[]{:S(2)}, u32[]{:S(2)}) collective-permute-start(bf16[8,4,2,32]{3,0,2,1:T(8,128)(2,1)S(1)} %bitcast.202), channel_id=1, source_target_pairs={{0,384},{32,416},{64,448},{96,480},{128,256},{160,288},{192,320},{... | collective-permute-start | bytes 12296 | tf_op jit(solution)/shard_map/ppermute | solution.py:116
  142.5 1.9 collective-permute-start.14
  144.4 7.7 %collective-permute-start.15 = (bf16[8,4,2,32]{3,0,2,1:T(8,128)(2,1)S(1)}, bf16[8,4,2,32]{3,0,2,1:T(8,128)(2,1)S(1)}, u32[]{:S(2)}, u32[]{:S(2)}) collective-permute-start(bf16[8,4,2,32]{3,0,2,1:T(8,128)(2,1)S(1)} %bitcast.200), channel_id=1, source_target_pairs={{0,448},{32,480},{64,384},{96,416},{128,320},{160,352},{192,256},{... | collective-permute-start | bytes 12296 | tf_op jit(solution)/shard_map/ppermute | solution.py:116
  152.2 4.6 %collective-permute-start.16 = (bf16[8,4,2,32]{3,0,2,1:T(8,128)(2,1)S(1)}, bf16[8,4,2,32]{3,0,2,1:T(8,128)(2,1)S(1)}, u32[]{:S(2)}, u32[]{:S(2)}) collective-permute-start(bf16[8,4,2,32]{3,0,2,1:T(8,128)(2,1)S(1)} %bitcast.199), channel_id=1, source_target_pairs={{0,480},{32,448},{64,416},{96,384},{128,352},{160,320},{192,288},{... | collective-permute-start | bytes 12296 | tf_op jit(solution)/shard_map/ppermute | solution.py:116
  156.9 4.3 %collective-permute-done.16 = bf16[8,4,2,32]{3,0,2,1:T(8,128)(2,1)S(1)} collective-permute-done((bf16[8,4,2,32]{3,0,2,1:T(8,128)(2,1)S(1)}, bf16[8,4,2,32]{3,0,2,1:T(8,128)(2,1)S(1)}, u32[]{:S(2)}, u32[]{:S(2)}) %collective-permute-start.16) | collective-permute-done | bytes 4128 | tf_op jit(solution)/shard_map/ppermute | solution.py:116
  161.2 0.6 gather_fusion
  161.8 0.3 copy.87
  163.0 1.9 collective-permute-start.17
  165.0 6.0 %collective-permute-start.18 = (bf16[8,1,4,256]{3,2,1,0:T(4,128)(2,1)S(1)}, bf16[8,1,4,256]{3,2,1,0:T(4,128)(2,1)S(1)}, u32[]{:S(2)}, u32[]{:S(2)}) collective-permute-start(bf16[8,1,4,256]{3,2,1,0:T(4,128)(2,1)S(1)} %get-tuple-element.38), channel_id=1, source_target_pairs={{32,0},{64,32},{96,64},{128,96},{160,128},{192,160},{224,192},{256... | collective-permute-start | bytes 49160 | tf_op jit(solution)/shard_map/ppermute | solution.py:26
  171.1 1.3 collective-permute-done.18
  172.6 1.9 collective-permute-start.20
  174.5 2.6 %collective-permute-start.19 = (bf16[8,10,1,256]{3,2,1,0:T(2,128)(2,1)S(1)}, bf16[8,10,1,256]{3,2,1,0:T(2,128)(2,1)S(1)}, u32[]{:S(2)}, u32[]{:S(2)}) collective-permute-start(bf16[8,10,1,256]{3,2,1,0:T(2,128)(2,1)S(1)} %get-tuple-element.36), channel_id=1, source_target_pairs={{0,1},{1,2},{2,3},{3,4},{4,5},{5,6},{6,7},{7,8},{8,9},{9,10},{10,1... | collective-permute-start | bytes 122888 | tf_op jit(solution)/shard_map/ppermute | solution.py:25
  177.5 3.9 %collective-permute-done.19 = bf16[8,10,1,256]{3,2,1,0:T(2,128)(2,1)S(1)} collective-permute-done((bf16[8,10,1,256]{3,2,1,0:T(2,128)(2,1)S(1)}, bf16[8,10,1,256]{3,2,1,0:T(2,128)(2,1)S(1)}, u32[]{:S(2)}, u32[]{:S(2)}) %collective-permute-start.19) | collective-permute-done | bytes 40992 | tf_op jit(solution)/shard_map/ppermute | solution.py:25
  181.7 0.8 slice_dynamic-update-slice_fusion.17
  182.5 0.8 slice_dynamic-update-slice_fusion.16
  183.3 0.8 slice_dynamic-update-slice_fusion.15
  184.1 0.8 slice_dynamic-update-slice_fusion.14
  184.9 0.8 slice_dynamic-update-slice_fusion.13
  185.7 0.8 slice_dynamic-update-slice_fusion.12
  186.5 0.8 slice_dynamic-update-slice_fusion.11
  187.2 0.8 slice_dynamic-update-slice_fusion.10
  188.0 0.8 slice_dynamic-update-slice_fusion.9
  188.8 3.3 %fusion.41 = (bf16[1,3,3,256,256]{3,4,2,1,0:T(8,128)(2,1)S(1)}, bf16[1,3,3,256,256]{3,4,2,1,0:T(8,128)(2,1)S(1)}, bf16[1,3,3,256,256]{3,4,2,1,0:T(8,128)(2,1)}) fusion(bf16[3,3,3,256,256]{3,4,2,1,0:T(8,128)(2,1)} %all-gather.5.cloned.1.call-done), kind=kLoop, calls=%fused_computation.161 | loop fusion | bytes 7077888 | tf_op jit(solution)/shard_map/slice | solution.py:66
  192.1 2.4 copy.107
  194.5 1.5 copy.108
  196.0 0.7 copy.109
  196.8 2.4 %fusion.49 = f32[8,8,4,256]{3,2,1,0:T(4,128)S(1)} fusion(bf16[10,8,4,2304]{3,2,1,0:T(4,128)(2,1)} %slice_dynamic-update-slice_fusion.9, bf16[2304,256,1,1]{1,0,3,2:T(8,128)(2,1)} %bitcast.187), kind=kOutput, calls=%fused_computation.169 | convolution fusion | flops 301989888 | bytes 2916352 | tf_op jit(solution)/shard_map/dot_general | solution.py:62
  199.2 2.0 convolution_add_fusion.3
  201.2 2.1 fusion.14
  204.0 6.3 %collective-permute-start.22 = (bf16[8,1,8,128]{3,2,1,0:T(8,128)(2,1)S(1)}, bf16[8,1,8,128]{3,2,1,0:T(8,128)(2,1)S(1)}, u32[]{:S(2)}, u32[]{:S(2)}) collective-permute-start(bf16[8,1,8,128]{3,2,1,0:T(8,128)(2,1)S(1)} %get-tuple-element.19), channel_id=1, source_target_pairs={{32,0},{64,32},{96,64},{128,96},{160,128},{192,160},{224,192},{256... | collective-permute-start | bytes 49160 | tf_op jit(solution)/shard_map/ppermute | solution.py:26
  210.3 1.9 collective-permute-start.21
  212.3 5.8 %collective-permute-done.21 = bf16[8,1,8,128]{3,2,1,0:T(8,128)(2,1)S(1)} collective-permute-done((bf16[8,1,8,128]{3,2,1,0:T(8,128)(2,1)S(1)}, bf16[8,1,8,128]{3,2,1,0:T(8,128)(2,1)S(1)}, u32[]{:S(2)}, u32[]{:S(2)}) %collective-permute-start.21) | collective-permute-done | bytes 16416 | tf_op jit(solution)/shard_map/ppermute | solution.py:25
  218.2 1.9 collective-permute-start.24
  220.1 2.4 %collective-permute-start.23 = (bf16[8,18,1,128]{3,2,1,0:T(2,128)(2,1)S(1)}, bf16[8,18,1,128]{3,2,1,0:T(2,128)(2,1)S(1)}, u32[]{:S(2)}, u32[]{:S(2)}) collective-permute-start(bf16[8,18,1,128]{3,2,1,0:T(2,128)(2,1)S(1)} %get-tuple-element.16), channel_id=1, source_target_pairs={{0,1},{1,2},{2,3},{3,4},{4,5},{5,6},{6,7},{7,8},{8,9},{9,10},{10,1... | collective-permute-start | bytes 110600 | tf_op jit(solution)/shard_map/ppermute | solution.py:25
  222.7 4.3 %collective-permute-done.23 = bf16[8,18,1,128]{3,2,1,0:T(2,128)(2,1)S(1)} collective-permute-done((bf16[8,18,1,128]{3,2,1,0:T(2,128)(2,1)S(1)}, bf16[8,18,1,128]{3,2,1,0:T(2,128)(2,1)S(1)}, u32[]{:S(2)}, u32[]{:S(2)}) %collective-permute-start.23) | collective-permute-done | bytes 36896 | tf_op jit(solution)/shard_map/ppermute | solution.py:25
  227.0 0.4 fusion.21
  228.7 0.8 fusion.50
  229.5 0.8 convolution_add_fusion.1
  230.5 1.5 fusion.12
  (111 shorter events, 4.7 us)
Async XLA Ops:
  7.4 155.0 %copy-start = (bf16[512,256]{1,0:T(8,128)(2,1)S(1)}, bf16[512,256]{1,0:T(8,128)(2,1)}, u32[]{:S(2)}) copy-start(bf16[512,256]{1,0:T(8,128)(2,1)} %param.10) | copy-start | bytes 786436
  7.4 71.5 %copy-start.2 = (bf16[3,3,3,512,32]{3,4,2,1,0:T(8,128)(2,1)S(1)}, bf16[3,3,3,512,32]{3,4,2,1,0:T(8,128)(2,1)}, u32[]{:S(2)}) copy-start(bf16[3,3,3,512,32]{3,4,2,1,0:T(8,128)(2,1)} %param.7) | copy-start | bytes 2654212
  7.4 64.1 %all-gather.3.cloned.1.call-start = ((), (), s32[]{:S(2)}) async-start(), calls=%async_computation | async-start | bytes 1114112 | tf_op jit(solution)/shard_map/all_gather | solution.py:107
  10.0 178.8 %all-gather.5.cloned.1.call-start = ((), (), s32[]{:S(2)}) async-start(), calls=%async_computation.1 | async-start | bytes 3649536 | tf_op jit(solution)/shard_map/all_gather | solution.py:102
  74.4 8.9 %collective-permute-start.1 = (bf16[8,64,1,512]{3,1,2,0:T(8,128)(2,1)}, bf16[8,64,1,512]{3,1,2,0:T(8,128)(2,1)S(1)}, u32[]{:S(2)}, u32[]{:S(2)}) collective-permute-start(bf16[8,64,1,512]{3,1,2,0:T(8,128)(2,1)} %get-tuple-element.9), channel_id=1, source_target_pairs={{1,0},{2,1},{3,2},{4,3},{5,4},{6,5},{7,6},{8,7},{9,8},{10,9},{11,1... | collective-permute-start | bytes 1572872 | tf_op jit(solution)/shard_map/ppermute | solution.py:26
  76.3 11.9 %collective-permute-start = (bf16[8,64,1,512]{3,1,2,0:T(8,128)(2,1)}, bf16[8,64,1,512]{3,1,2,0:T(8,128)(2,1)S(1)}, u32[]{:S(2)}, u32[]{:S(2)}) collective-permute-start(bf16[8,64,1,512]{3,1,2,0:T(8,128)(2,1)} %get-tuple-element.8), channel_id=1, source_target_pairs={{0,1},{1,2},{2,3},{3,4},{4,5},{5,6},{6,7},{7,8},{8,9},{9,10},{10,1... | collective-permute-start | bytes 1572872 | tf_op jit(solution)/shard_map/ppermute | solution.py:25
  96.1 66.3 %copy-start.4 = (bf16[8,4,2,512]{3,2,1,0:T(2,128)(2,1)S(1)}, bf16[8,4,2,512]{3,2,1,0:T(2,128)(2,1)}, u32[]{:S(2)}) copy-start(bf16[8,4,2,512]{3,2,1,0:T(2,128)(2,1)} %param.6) | copy-start | bytes 196612
  96.3 15.2 %collective-permute-start.2 = (bf16[8,4,2,32]{3,0,2,1:T(8,128)(2,1)S(1)}, bf16[8,4,2,32]{3,0,2,1:T(8,128)(2,1)S(1)}, u32[]{:S(2)}, u32[]{:S(2)}) collective-permute-start(bf16[8,4,2,32]{3,0,2,1:T(8,128)(2,1)S(1)} %bitcast.213), channel_id=1, source_target_pairs={{0,32},{32,0},{64,96},{96,64},{128,160},{160,128},{192,224},{224,1... | collective-permute-start | bytes 12296 | tf_op jit(solution)/shard_map/ppermute | solution.py:116
  98.5 18.6 %collective-permute-start.3 = (bf16[8,4,2,32]{3,0,2,1:T(8,128)(2,1)S(1)}, bf16[8,4,2,32]{3,0,2,1:T(8,128)(2,1)S(1)}, u32[]{:S(2)}, u32[]{:S(2)}) collective-permute-start(bf16[8,4,2,32]{3,0,2,1:T(8,128)(2,1)S(1)} %bitcast.212), channel_id=1, source_target_pairs={{0,64},{32,96},{64,0},{96,32},{128,192},{160,224},{192,128},{224,1... | collective-permute-start | bytes 12296 | tf_op jit(solution)/shard_map/ppermute | solution.py:116
  102.6 19.1 %collective-permute-start.4 = (bf16[8,4,2,32]{3,0,2,1:T(8,128)(2,1)S(1)}, bf16[8,4,2,32]{3,0,2,1:T(8,128)(2,1)S(1)}, u32[]{:S(2)}, u32[]{:S(2)}) collective-permute-start(bf16[8,4,2,32]{3,0,2,1:T(8,128)(2,1)S(1)} %bitcast.211), channel_id=1, source_target_pairs={{0,96},{32,64},{64,32},{96,0},{128,224},{160,192},{192,160},{224,1... | collective-permute-start | bytes 12296 | tf_op jit(solution)/shard_map/ppermute | solution.py:116
  106.8 18.3 %collective-permute-start.5 = (bf16[8,4,2,32]{3,0,2,1:T(8,128)(2,1)S(1)}, bf16[8,4,2,32]{3,0,2,1:T(8,128)(2,1)S(1)}, u32[]{:S(2)}, u32[]{:S(2)}) collective-permute-start(bf16[8,4,2,32]{3,0,2,1:T(8,128)(2,1)S(1)} %bitcast.210), channel_id=1, source_target_pairs={{0,128},{32,160},{64,192},{96,224},{128,0},{160,32},{192,64},{224,... | collective-permute-start | bytes 12296 | tf_op jit(solution)/shard_map/ppermute | solution.py:116
  109.4 17.6 %collective-permute-start.6 = (bf16[8,4,2,32]{3,0,2,1:T(8,128)(2,1)S(1)}, bf16[8,4,2,32]{3,0,2,1:T(8,128)(2,1)S(1)}, u32[]{:S(2)}, u32[]{:S(2)}) collective-permute-start(bf16[8,4,2,32]{3,0,2,1:T(8,128)(2,1)S(1)} %bitcast.209), channel_id=1, source_target_pairs={{0,160},{32,128},{64,224},{96,192},{128,32},{160,0},{192,96},{224,... | collective-permute-start | bytes 12296 | tf_op jit(solution)/shard_map/ppermute | solution.py:116
  111.5 22.8 %collective-permute-start.7 = (bf16[8,4,2,32]{3,0,2,1:T(8,128)(2,1)S(1)}, bf16[8,4,2,32]{3,0,2,1:T(8,128)(2,1)S(1)}, u32[]{:S(2)}, u32[]{:S(2)}) collective-permute-start(bf16[8,4,2,32]{3,0,2,1:T(8,128)(2,1)S(1)} %bitcast.208), channel_id=1, source_target_pairs={{0,192},{32,224},{64,128},{96,160},{128,64},{160,96},{192,0},{224,... | collective-permute-start | bytes 12296 | tf_op jit(solution)/shard_map/ppermute | solution.py:116
  117.1 22.4 %collective-permute-start.8 = (bf16[8,4,2,32]{3,0,2,1:T(8,128)(2,1)S(1)}, bf16[8,4,2,32]{3,0,2,1:T(8,128)(2,1)S(1)}, u32[]{:S(2)}, u32[]{:S(2)}) collective-permute-start(bf16[8,4,2,32]{3,0,2,1:T(8,128)(2,1)S(1)} %bitcast.207), channel_id=1, source_target_pairs={{0,224},{32,192},{64,160},{96,128},{128,96},{160,64},{192,32},{224... | collective-permute-start | bytes 12296 | tf_op jit(solution)/shard_map/ppermute | solution.py:116
  121.7 20.8 %collective-permute-start.9 = (bf16[8,4,2,32]{3,0,2,1:T(8,128)(2,1)S(1)}, bf16[8,4,2,32]{3,0,2,1:T(8,128)(2,1)S(1)}, u32[]{:S(2)}, u32[]{:S(2)}) collective-permute-start(bf16[8,4,2,32]{3,0,2,1:T(8,128)(2,1)S(1)} %bitcast.206), channel_id=1, source_target_pairs={{0,256},{32,288},{64,320},{96,352},{128,384},{160,416},{192,448},{... | collective-permute-start | bytes 12296 | tf_op jit(solution)/shard_map/ppermute | solution.py:116
  125.1 19.3 %collective-permute-start.10 = (bf16[8,4,2,32]{3,0,2,1:T(8,128)(2,1)S(1)}, bf16[8,4,2,32]{3,0,2,1:T(8,128)(2,1)S(1)}, u32[]{:S(2)}, u32[]{:S(2)}) collective-permute-start(bf16[8,4,2,32]{3,0,2,1:T(8,128)(2,1)S(1)} %bitcast.205), channel_id=1, source_target_pairs={{0,288},{32,256},{64,352},{96,320},{128,416},{160,384},{192,480},{... | collective-permute-start | bytes 12296 | tf_op jit(solution)/shard_map/ppermute | solution.py:116
  127.1 25.1 %collective-permute-start.11 = (bf16[8,4,2,32]{3,0,2,1:T(8,128)(2,1)S(1)}, bf16[8,4,2,32]{3,0,2,1:T(8,128)(2,1)S(1)}, u32[]{:S(2)}, u32[]{:S(2)}) collective-permute-start(bf16[8,4,2,32]{3,0,2,1:T(8,128)(2,1)S(1)} %bitcast.204), channel_id=1, source_target_pairs={{0,320},{32,352},{64,256},{96,288},{128,448},{160,480},{192,384},{... | collective-permute-start | bytes 12296 | tf_op jit(solution)/shard_map/ppermute | solution.py:116
  134.3 22.5 %collective-permute-start.12 = (bf16[8,4,2,32]{3,0,2,1:T(8,128)(2,1)S(1)}, bf16[8,4,2,32]{3,0,2,1:T(8,128)(2,1)S(1)}, u32[]{:S(2)}, u32[]{:S(2)}) collective-permute-start(bf16[8,4,2,32]{3,0,2,1:T(8,128)(2,1)S(1)} %bitcast.203), channel_id=1, source_target_pairs={{0,352},{32,320},{64,288},{96,256},{128,480},{160,448},{192,416},{... | collective-permute-start | bytes 12296 | tf_op jit(solution)/shard_map/ppermute | solution.py:116
  139.6 17.3 %collective-permute-start.13 = (bf16[8,4,2,32]{3,0,2,1:T(8,128)(2,1)S(1)}, bf16[8,4,2,32]{3,0,2,1:T(8,128)(2,1)S(1)}, u32[]{:S(2)}, u32[]{:S(2)}) collective-permute-start(bf16[8,4,2,32]{3,0,2,1:T(8,128)(2,1)S(1)} %bitcast.202), channel_id=1, source_target_pairs={{0,384},{32,416},{64,448},{96,480},{128,256},{160,288},{192,320},{... | collective-permute-start | bytes 12296 | tf_op jit(solution)/shard_map/ppermute | solution.py:116
  142.5 14.3 %collective-permute-start.14 = (bf16[8,4,2,32]{3,0,2,1:T(8,128)(2,1)S(1)}, bf16[8,4,2,32]{3,0,2,1:T(8,128)(2,1)S(1)}, u32[]{:S(2)}, u32[]{:S(2)}) collective-permute-start(bf16[8,4,2,32]{3,0,2,1:T(8,128)(2,1)S(1)} %bitcast.201), channel_id=1, source_target_pairs={{0,416},{32,384},{64,480},{96,448},{128,288},{160,256},{192,352},{... | collective-permute-start | bytes 12296 | tf_op jit(solution)/shard_map/ppermute | solution.py:116
  144.4 12.4 %collective-permute-start.15 = (bf16[8,4,2,32]{3,0,2,1:T(8,128)(2,1)S(1)}, bf16[8,4,2,32]{3,0,2,1:T(8,128)(2,1)S(1)}, u32[]{:S(2)}, u32[]{:S(2)}) collective-permute-start(bf16[8,4,2,32]{3,0,2,1:T(8,128)(2,1)S(1)} %bitcast.200), channel_id=1, source_target_pairs={{0,448},{32,480},{64,384},{96,416},{128,320},{160,352},{192,256},{... | collective-permute-start | bytes 12296 | tf_op jit(solution)/shard_map/ppermute | solution.py:116
  152.2 9.0 %collective-permute-start.16 = (bf16[8,4,2,32]{3,0,2,1:T(8,128)(2,1)S(1)}, bf16[8,4,2,32]{3,0,2,1:T(8,128)(2,1)S(1)}, u32[]{:S(2)}, u32[]{:S(2)}) collective-permute-start(bf16[8,4,2,32]{3,0,2,1:T(8,128)(2,1)S(1)} %bitcast.199), channel_id=1, source_target_pairs={{0,480},{32,448},{64,416},{96,384},{128,352},{160,320},{192,288},{... | collective-permute-start | bytes 12296 | tf_op jit(solution)/shard_map/ppermute | solution.py:116
  163.0 8.0 %collective-permute-start.17 = (bf16[8,1,4,256]{3,2,1,0:T(4,128)(2,1)S(1)}, bf16[8,1,4,256]{3,2,1,0:T(4,128)(2,1)S(1)}, u32[]{:S(2)}, u32[]{:S(2)}) collective-permute-start(bf16[8,1,4,256]{3,2,1,0:T(4,128)(2,1)S(1)} %get-tuple-element.39), channel_id=1, source_target_pairs={{0,32},{32,64},{64,96},{96,128},{128,160},{160,192},{192,224},{224... | collective-permute-start | bytes 49160 | tf_op jit(solution)/shard_map/ppermute | solution.py:25
  165.0 7.5 %collective-permute-start.18 = (bf16[8,1,4,256]{3,2,1,0:T(4,128)(2,1)S(1)}, bf16[8,1,4,256]{3,2,1,0:T(4,128)(2,1)S(1)}, u32[]{:S(2)}, u32[]{:S(2)}) collective-permute-start(bf16[8,1,4,256]{3,2,1,0:T(4,128)(2,1)S(1)} %get-tuple-element.38), channel_id=1, source_target_pairs={{32,0},{64,32},{96,64},{128,96},{160,128},{192,160},{224,192},{256... | collective-permute-start | bytes 49160 | tf_op jit(solution)/shard_map/ppermute | solution.py:26
  172.6 4.9 %collective-permute-start.20 = (bf16[8,10,1,256]{3,2,1,0:T(2,128)(2,1)S(1)}, bf16[8,10,1,256]{3,2,1,0:T(2,128)(2,1)S(1)}, u32[]{:S(2)}, u32[]{:S(2)}) collective-permute-start(bf16[8,10,1,256]{3,2,1,0:T(2,128)(2,1)S(1)} %get-tuple-element.37), channel_id=1, source_target_pairs={{1,0},{2,1},{3,2},{4,3},{5,4},{6,5},{7,6},{8,7},{9,8},{10,9},{11,1... | collective-permute-start | bytes 122888 | tf_op jit(solution)/shard_map/ppermute | solution.py:26
  174.5 7.0 %collective-permute-start.19 = (bf16[8,10,1,256]{3,2,1,0:T(2,128)(2,1)S(1)}, bf16[8,10,1,256]{3,2,1,0:T(2,128)(2,1)S(1)}, u32[]{:S(2)}, u32[]{:S(2)}) collective-permute-start(bf16[8,10,1,256]{3,2,1,0:T(2,128)(2,1)S(1)} %get-tuple-element.36), channel_id=1, source_target_pairs={{0,1},{1,2},{2,3},{3,4},{4,5},{5,6},{6,7},{7,8},{8,9},{9,10},{10,1... | collective-permute-start | bytes 122888 | tf_op jit(solution)/shard_map/ppermute | solution.py:25
  196.8 2.4 %copy-start.1 = (bf16[1,3,3,256,256]{4,3,2,1,0:T(8,128)(2,1)S(1)}, bf16[1,3,3,256,256]{4,3,2,1,0:T(8,128)(2,1)}, u32[]{:S(2)}) copy-start(bf16[1,3,3,256,256]{4,3,2,1,0:T(8,128)(2,1)} %copy.108) | copy-start | bytes 3538948
  201.2 2.1 copy-start.5
  201.2 21.3 %copy-start.3 = (bf16[3,3,3,128,128]{4,3,2,1,0:T(8,128)(2,1)S(1)}, bf16[3,3,3,128,128]{4,3,2,1,0:T(8,128)(2,1)}, u32[]{:S(2)}) copy-start(bf16[3,3,3,128,128]{4,3,2,1,0:T(8,128)(2,1)} %param.9) | copy-start | bytes 2654212
  204.0 8.3 %collective-permute-start.22 = (bf16[8,1,8,128]{3,2,1,0:T(8,128)(2,1)S(1)}, bf16[8,1,8,128]{3,2,1,0:T(8,128)(2,1)S(1)}, u32[]{:S(2)}, u32[]{:S(2)}) collective-permute-start(bf16[8,1,8,128]{3,2,1,0:T(8,128)(2,1)S(1)} %get-tuple-element.19), channel_id=1, source_target_pairs={{32,0},{64,32},{96,64},{128,96},{160,128},{192,160},{224,192},{256... | collective-permute-start | bytes 49160 | tf_op jit(solution)/shard_map/ppermute | solution.py:26
  210.3 7.7 %collective-permute-start.21 = (bf16[8,1,8,128]{3,2,1,0:T(8,128)(2,1)S(1)}, bf16[8,1,8,128]{3,2,1,0:T(8,128)(2,1)S(1)}, u32[]{:S(2)}, u32[]{:S(2)}) collective-permute-start(bf16[8,1,8,128]{3,2,1,0:T(8,128)(2,1)S(1)} %get-tuple-element.18), channel_id=1, source_target_pairs={{0,32},{32,64},{64,96},{96,128},{128,160},{160,192},{192,224},{224... | collective-permute-start | bytes 49160 | tf_op jit(solution)/shard_map/ppermute | solution.py:25
  218.2 4.5 %collective-permute-start.24 = (bf16[8,18,1,128]{3,2,1,0:T(2,128)(2,1)S(1)}, bf16[8,18,1,128]{3,2,1,0:T(2,128)(2,1)S(1)}, u32[]{:S(2)}, u32[]{:S(2)}) collective-permute-start(bf16[8,18,1,128]{3,2,1,0:T(2,128)(2,1)S(1)} %get-tuple-element.17), channel_id=1, source_target_pairs={{1,0},{2,1},{3,2},{4,3},{5,4},{6,5},{7,6},{8,7},{9,8},{10,9},{11,1... | collective-permute-start | bytes 110600 | tf_op jit(solution)/shard_map/ppermute | solution.py:26
  220.1 6.9 %collective-permute-start.23 = (bf16[8,18,1,128]{3,2,1,0:T(2,128)(2,1)S(1)}, bf16[8,18,1,128]{3,2,1,0:T(2,128)(2,1)S(1)}, u32[]{:S(2)}, u32[]{:S(2)}) collective-permute-start(bf16[8,18,1,128]{3,2,1,0:T(2,128)(2,1)S(1)} %get-tuple-element.16), channel_id=1, source_target_pairs={{0,1},{1,2},{2,3},{3,4},{4,5},{5,6},{6,7},{7,8},{8,9},{9,10},{10,1... | collective-permute-start | bytes 110600 | tf_op jit(solution)/shard_map/ppermute | solution.py:25
Sparse Core Ops, SparseCore 0:
  11.2 60.2 all-gather.2
Sparse Core Ops, SparseCore 1:
  78.8 75.0 all-gather.4
